TPU v7x, 32 devices: a whole 2x2x4 slice. The times are simulated.
32 devices in a mesh: wide: 8 (over y, x, core), blk: 4 (over z).
Axes of the slice: x: 2, y: 2, z: 4, core: 2. Of those that a mesh axis runs over, the one named last changes fastest.
Arguments:
- hidden: bfloat16 [4, 64, 8192], P('blk', 'wide'), may hold values from -400 to 400, as said below
- norm_gain: float32 [8192], replicated, may hold values from 0.1 to 1.9
- w_query: bfloat16 [8192, 8192], P('blk', 'wide'), may hold values from -0.0625 to 0.0625
- key_weight_matrix: bfloat16 [8192, 1024], P('blk'), may hold values from -0.0625 to 0.0625
- value_weight_matrix: bfloat16 [8192, 1024], P('blk'), may hold values from -0.0625 to 0.0625
- cache_key: bfloat16 [8192, 1024], P('blk'), may hold values from -90 to 90
- prefix_value_cache: bfloat16 [8192, 1024], P('blk'), may hold values from -5 to 5
- start: int32 [1], replicated, may hold values from 8192 to 130816
- reach: int32 [4, 64], P('blk'), may hold values from 0 to 8447
- passkey: int32 [16], replicated, may hold values from 0 to 8191
Outputs:
- attended: bfloat16 [4, 64, 8192], P('blk', 'wide')
Inputs may be any that keep to these rules, and one draw needn't show every extreme that they name: hidden states of order one up to row and feature scales.
All inputs are finite; a program needn't handle non-finite values.
Results may differ from a plain program's by a relative error of at most 0.017.
The roundings to bfloat16 on the way count: a program that leaves them out, or rounds other values in their place, can miss the bound.
Values may be sent and summed in bfloat16 or wider, within the bound.
No kernel may reach another device: no remote copies, remote signals or barrier semaphores. Data moves between devices by JAX's collectives and lax.ppermute only.
A program may use at most 128 MiB of HBM per device.

v0:
```python
import math
import jax
import jax.numpy as jnp
from jax import lax
from jax.sharding import PartitionSpec as P

QUERY_HEADS = 64
KEY_VALUE_HEADS = 8
HEAD_WIDTH = 128
rope_base = 500000.0
yarn_factor = 8.0
trained_context = 8192.0
fast_turns = 32.0
slow_turns = 1.0
masked_score = -1e30


def shifted(block, axis, distance):
    devices = range(lax.axis_size(axis))
    route = [((i - distance) % len(devices), i) for i in devices]
    return lax.ppermute(block, axis, route)


def yarn_tables(positions, head_size):
    half = head_size // 2
    log_base = math.log(rope_base)
    lowest = math.floor(
        head_size * math.log(trained_context / (fast_turns * 2.0 * math.pi)) / (2.0 * log_base)
    )
    highest = math.ceil(
        head_size * math.log(trained_context / (slow_turns * 2.0 * math.pi)) / (2.0 * log_base)
    )
    spread = max(highest - lowest, 1)
    counter = jnp.arange(half, dtype=jnp.float32)
    inverse = jnp.exp(-(2.0 * counter / head_size) * log_base)
    ramp = jnp.clip((counter - lowest) / spread, 0.0, 1.0)
    mixed = inverse / yarn_factor * ramp + inverse * (1.0 - ramp)
    angles = positions.astype(jnp.float32)[:, None] * mixed[None, :]
    mscale = 0.1 * math.log(yarn_factor) + 1.0
    return (jnp.cos(angles) * mscale, jnp.sin(angles) * mscale)


def apply_rotary(matrix, heads, cosine_table, sine_table):
    count = matrix.shape[0]
    shaped = matrix.reshape(count, heads, -1)
    half = shaped.shape[2] // 2
    front = shaped[:, :, :half]
    back = shaped[:, :, half:]
    cosine_table = cosine_table[:, None, :]
    sine_table = sine_table[:, None, :]
    turned = jnp.concatenate(
        [front * cosine_table - back * sine_table, back * cosine_table + front * sine_table], axis=2
    )
    return turned.reshape(count, heads * 2 * half)


def local(
    hidden,
    norm_gain,
    w_query,
    key_weight_matrix,
    value_weight_matrix,
    cache_key,
    prefix_value_cache,
    start,
    reach,
    passkey,
):
    blocks = lax.axis_size("blk")
    groups = lax.axis_size("wide")
    block_id = lax.axis_index("blk")
    group_number = lax.axis_index("wide")
    qcols = w_query.shape[1]
    query_head_rows = QUERY_HEADS // groups
    head_of_value = group_number * query_head_rows // (QUERY_HEADS // KEY_VALUE_HEADS)
    tokens = hidden[0].astype(jnp.float32)
    inv_rms = lax.rsqrt(jnp.mean(tokens * tokens, axis=1, keepdims=True) + 1e-05)
    normed = (tokens * inv_rms * norm_gain[None, :]).astype(jnp.bfloat16)[None]
    head_base = head_of_value * HEAD_WIDTH
    key_cols = lax.dynamic_slice_in_dim(key_weight_matrix, head_base, HEAD_WIDTH, 1)
    value_cols = lax.dynamic_slice_in_dim(value_weight_matrix, head_base, HEAD_WIDTH, 1)
    kv_width = key_cols.shape[1]
    sliced = lax.all_to_all(normed, "blk", split_axis=2, concat_axis=0, tiled=True)
    spread = lax.all_gather(sliced, "wide", axis=1, tiled=True)
    local_weights = jnp.concatenate([w_query, key_cols, value_cols], axis=1)
    summed = lax.psum_scatter(
        jnp.einsum("btd,dc->btc", spread, local_weights, preferred_element_type=jnp.float32),
        "blk",
        scatter_dimension=0,
        tiled=True,
    )[0]
    query_raw = summed[:, :qcols]
    unrotated_key = summed[:, qcols : qcols + kv_width]
    value_raw = summed[:, qcols + kv_width :]
    tokens_block = summed.shape[0]
    positions = start[0] + block_id * tokens_block + jnp.arange(tokens_block, dtype=jnp.int32)
    cosine_table, sine_table = yarn_tables(positions, HEAD_WIDTH)
    query = apply_rotary(query_raw, query_head_rows, cosine_table, sine_table).astype(jnp.bfloat16)
    window_key_rows = apply_rotary(unrotated_key, 1, cosine_table, sine_table).astype(jnp.bfloat16)
    value_new = value_raw.astype(jnp.bfloat16)
    queries = (
        query.reshape(tokens_block, query_head_rows, HEAD_WIDTH)
        .transpose(1, 0, 2)
        .reshape(query_head_rows * tokens_block, HEAD_WIDTH)
    )
    cache_rows = cache_key.shape[0]
    cache_total = cache_rows * blocks
    own_index = cache_total + block_id * tokens_block + jnp.arange(tokens_block, dtype=jnp.int32)
    query_index = jnp.tile(own_index, query_head_rows)
    query_reach = jnp.tile(reach[0], query_head_rows)
    cache_keys = lax.dynamic_slice_in_dim(cache_key, head_base, HEAD_WIDTH, 1)
    cache_values = lax.dynamic_slice_in_dim(prefix_value_cache, head_base, HEAD_WIDTH, 1)
    key_block = jnp.concatenate([cache_keys, window_key_rows], axis=0)
    value_block = jnp.concatenate([cache_values, value_new], axis=0)
    pair_block = jnp.stack([key_block, value_block], axis=0)[None]
    pair_len = cache_rows + tokens_block
    inv_sqrt = 1.0 / math.sqrt(HEAD_WIDTH)

    def attend(carry, pieces, first_operand):
        best, total, summed_values = carry
        count = pieces.shape[0]
        source = first_operand + jnp.arange(count, dtype=jnp.int32)[:, None]
        offset = jnp.arange(pair_len, dtype=jnp.int32)[None, :]
        in_cache = offset < cache_rows
        cache_index = source * cache_rows + offset
        key_index = jnp.where(
            in_cache, cache_index, cache_total + source * tokens_block + offset - cache_rows
        )
        pinned = in_cache & jnp.any(cache_index[:, :, None] == passkey[None, None, :], axis=2)
        key_index = key_index.reshape(count * pair_len)
        pinned = pinned.reshape(count * pair_len)
        keys_flat = pieces[:, 0].reshape(count * pair_len, HEAD_WIDTH)
        values_flat = pieces[:, 1].reshape(count * pair_len, HEAD_WIDTH)
        scores = (
            lax.dot_general(
                queries, keys_flat, (((1,), (1,)), ((), ())), preferred_element_type=jnp.float32
            )
            * inv_sqrt
        )
        visible = (key_index[None, :] <= query_index[:, None]) & (
            (key_index[None, :] >= query_index[:, None] - query_reach[:, None]) | pinned[None, :]
        )
        scores = jnp.where(visible, scores, masked_score)
        fresh = jnp.maximum(best, jnp.max(scores, axis=1))
        decay = jnp.exp(best - fresh)
        weights = jnp.where(visible, jnp.exp(scores - fresh[:, None]), 0.0)
        total = total * decay + jnp.sum(weights, axis=1)
        summed_values = summed_values * decay[:, None] + jnp.dot(
            weights.astype(jnp.bfloat16), values_flat, preferred_element_type=jnp.float32
        )
        return (fresh, total, summed_values)

    query_rows = query_head_rows * tokens_block
    initial_state = (
        jnp.full((query_rows,), masked_score, jnp.float32),
        jnp.zeros((query_rows,), jnp.float32),
        jnp.zeros((query_rows, HEAD_WIDTH), jnp.float32),
    )
    state = attend(initial_state, pair_block, block_id)

    def turn(step, loop_state):
        carry, travelling = loop_state
        travelling = shifted(travelling, "blk", 1)
        source_block = (block_id - step - 1) % blocks
        return (attend(carry, travelling, source_block), travelling)

    state, _ = lax.fori_loop(0, blocks - 1, turn, (state, pair_block))
    best, total, summed_values = state
    heads_out = (summed_values / total[:, None]).astype(jnp.bfloat16)
    heads_out = (
        heads_out.reshape(query_head_rows, tokens_block, HEAD_WIDTH)
        .transpose(1, 0, 2)
        .reshape(1, tokens_block, qcols)
    )
    return lax.all_to_all(heads_out, "wide", split_axis=1, concat_axis=2, tiled=True)


def solution(mesh):
    return jax.shard_map(
        local,
        mesh=mesh,
        in_specs=(
            P("blk", "wide", None),
            P(),
            P("blk", "wide"),
            P("blk", None),
            P("blk", None),
            P("blk", None),
            P("blk", None),
            P(),
            P("blk", None),
            P(),
        ),
        out_specs=P("blk", "wide", None),
        check_vma=False,
    )
```

profile of v0, /device:TPU:0, one launch (start us, length us, event | category | flops | bytes accessed | tf_op | source)
XLA Modules:
  0.0 274.0 jit_solution(11445664194508917927)
XLA Ops:
  6.5 1.1 fusion.32
  7.6 1.0 fusion.34
  8.6 6.7 %copy.39 = bf16[1,8,8192]{1,0,2:T(2,128)(2,1)} copy(bf16[1,8,8192]{2,1,0:T(8,128)(2,1)S(1)} %fusion.34) | data formatting | bytes 262144 | tf_op jit(solution)/shard_map/convert_element_type | solution.py:78
  15.9 45.2 %reduce.8 = bf16[8192,8]{1,0:T(8,128)(2,1)S(1)} reduce(bf16[8192,1,8]{2,1,0:T(2,128)(2,1)} %bitcast.67, bf16[]{:T(256)} %broadcast.420), dimensions={1}, to_apply=%bitcast.49.reduce_sub_computation | reduce | bytes 262146
  61.1 2.2 reshape.416
  63.3 12.2 %all_to_all.36 = bf16[4,2,8192]{2,1,0:T(2,128)(2,1)S(1)} all-to-all(bf16[4,2,8192]{2,1,0:T(2,128)(2,1)S(1)} %reshape.416), channel_id=1, replica_groups=mesh['wide'=8,'blk'=4] {'blk'}, dimensions={0} | all-to-all | bytes 262144 | tf_op jit(solution)/shard_map/all_to_all | solution.py:83
  75.5 5.9 %reshape.417 = bf16[8192,1,8]{2,1,0:T(2,128)(2,1)} reshape(bf16[4,2,8192]{2,1,0:T(2,128)(2,1)S(1)} %all_to_all.36) | data formatting | bytes 262144
  81.4 8.6 %copy.40 = bf16[1,8,8192]{2,1,0:T(8,128)(2,1)} copy(bf16[1,8,8192]{1,0,2:T(2,128)(2,1)} %bitcast.68) | data formatting | bytes 262144 | tf_op jit(solution)/shard_map/all_to_all | solution.py:83
  90.2 1.3 constant_dynamic-slice_fusion.2
  91.6 21.2 %all-gather.3.cloned.1.call-done = bf16[4,1,64,2048]{3,2,0,1:T(8,128)(2,1)} async-done(((bf16[4,1,8,2048]{3,2,0,1:T(8,128)(2,1)}), bf16[4,1,64,2048]{3,2,0,1:T(8,128)(2,1)}) %all-gather.3.cloned.1.call-update) | async-done | bytes 1048592 | tf_op jit(solution)/shard_map/all_gather | solution.py:84
  112.7 5.1 %fusion.16 = f32[4,64,1280]{2,1,0:T(8,128)} fusion(bf16[2048,128]{1,0:T(8,128)(2,1)S(1)} %get-tuple-element.317, bf16[2048,128]{1,0:T(8,128)(2,1)S(1)} %get-tuple-element.318, bf16[2048,1024]{1,0:T(8,128)(2,1)} %param.14, bf16[4,1,64,2048]{3,2,0,1:T(8,128)(2,1)} %all-gather.3.cloned.1.call-done), kind=kOutput, calls=%fused_computation.23 | convolution fusion | flops 1357905920 | bytes 7602176 | tf_op jit(solution)/shard_map/btd,dc->btc/dot_general | solution.py:87
  119.1 1.3 constant_dynamic-slice_fusion
  120.4 28.9 %reduce-scatter.2.cloned.1.call-done = f32[1,64,1280]{2,1,0:T(8,128)} async-done(((f32[4,64,1280]{2,1,0:T(8,128)}), f32[1,64,1280]{2,1,0:T(8,128)}) %reduce-scatter.2.cloned.1.call-update) | async-done | bytes 327696 | tf_op jit(solution)/shard_map/reduce_scatter | solution.py:86
  150.8 1.0 slice_bitcast_fusion.8
  152.6 1.6 fusion.57
  154.2 2.2 fusion.23
  156.4 2.0 fusion.28
  158.4 97.2 %while.22 = (s32[]{:T(128)}, f32[512]{0:T(512)S(1)}, f32[512]{0:T(512)S(1)}, f32[512,128]{1,0:T(8,128)S(1)}, bf16[1,2,2112,128]{3,2,1,0:T(8,128)(2,1)S(1)}, /*in...) while((s32[]{:T(128)}, f32[512]{0:T(512)S(1)}, ...), condition=%wide.region_9.10_spmd.clone, body=%wide.region_5.9_spmd.clone.sunk | while | flops 576570880 | bytes 21332160 | solution.py:167
  158.8 26.9 %collective-permute-done = bf16[1,2,2112,128]{3,2,1,0:T(8,128)(2,1)S(1)} collective-permute-done((bf16[1,2,2112,128]{3,2,1,0:T(8,128)(2,1)S(1)}, bf16[1,2,2112,128]{3,2,1,0:T(8,128)(2,1)S(1)}, u32[]{:S(2)}, u32[]{:S(2)}) %collective-permute-start) | collective-permute-done | bytes 1081376 | tf_op jit(solution)/shard_map/while/body/eval_jaxpr/ppermute | solution.py:21
  185.7 1.6 fusion.69
  187.3 2.2 fusion.70
  189.6 2.1 fusion.71
  192.1 26.0 %collective-permute-done = bf16[1,2,2112,128]{3,2,1,0:T(8,128)(2,1)S(1)} collective-permute-done((bf16[1,2,2112,128]{3,2,1,0:T(8,128)(2,1)S(1)}, bf16[1,2,2112,128]{3,2,1,0:T(8,128)(2,1)S(1)}, u32[]{:S(2)}, u32[]{:S(2)}) %collective-permute-start) | collective-permute-done | bytes 1081376 | tf_op jit(solution)/shard_map/while/body/eval_jaxpr/ppermute | solution.py:21
  218.1 1.6 fusion.69
  219.7 2.2 fusion.70
  222.0 2.1 fusion.71
  224.5 25.1 %collective-permute-done = bf16[1,2,2112,128]{3,2,1,0:T(8,128)(2,1)S(1)} collective-permute-done((bf16[1,2,2112,128]{3,2,1,0:T(8,128)(2,1)S(1)}, bf16[1,2,2112,128]{3,2,1,0:T(8,128)(2,1)S(1)}, u32[]{:S(2)}, u32[]{:S(2)}) %collective-permute-start) | collective-permute-done | bytes 1081376 | tf_op jit(solution)/shard_map/while/body/eval_jaxpr/ppermute | solution.py:21
  249.6 1.6 fusion.69
  251.2 2.2 fusion.70
  253.5 2.1 fusion.71
  255.9 1.4 reduce.9
  257.4 9.0 %all_to_all.37 = bf16[8,2,4096]{2,1,0:T(2,128)(2,1)S(1)} all-to-all(bf16[8,2,4096]{2,1,0:T(2,128)(2,1)S(1)} %reshape.418), channel_id=1, replica_groups=mesh['wide'=8,'blk'=4] {'wide'}, dimensions={0} | all-to-all | bytes 262144 | tf_op jit(solution)/shard_map/all_to_all | solution.py:175
  (80 shorter events, 6.1 us)
Async XLA Ops:
  6.5 106.2 %all-gather.3.cloned.1.call-start = ((), (), s32[]{:S(2)}) async-start(), calls=%async_computation.4 | async-start | bytes 1179648 | tf_op jit(solution)/shard_map/all_gather | solution.py:84
  90.0 59.3 %reduce-scatter.2.cloned.1.call-start = ((), (), s32[]{:S(2)}) async-start(), calls=%async_computation.3 | async-start | bytes 1638400 | tf_op jit(solution)/shard_map/reduce_scatter | solution.py:86
  112.7 5.8 %copy-start.1 = (s32[1,64]{1,0:T(1,128)S(1)}, s32[1,64]{1,0:T(1,128)}, u32[]{:S(2)}) copy-start(s32[1,64]{1,0:T(1,128)} %param.20) | copy-start | bytes 772
  112.7 6.0 %copy-start = (s32[16]{0:T(128)S(1)}, s32[16]{0:T(128)}, u32[]{:S(2)}) copy-start(s32[16]{0:T(128)} %param.21) | copy-start | bytes 196
  158.4 27.3 %collective-permute-start = (bf16[1,2,2112,128]{3,2,1,0:T(8,128)(2,1)S(1)}, bf16[1,2,2112,128]{3,2,1,0:T(8,128)(2,1)S(1)}, u32[]{:S(2)}, u32[]{:S(2)}) collective-permute-start(bf16[1,2,2112,128]{3,2,1,0:T(8,128)(2,1)S(1)} %get-tuple-element.414), channel_id=1, source_target_pairs={{3,0},{0,1},{1,2},{2,3},{7,4},{4,5},{5,6},{6,7},{11,8},{8,9},{9,10... | collective-permute-start | bytes 3244040 | tf_op jit(solution)/shard_map/while/body/eval_jaxpr/ppermute | solution.py:21
  191.7 26.4 %collective-permute-start = (bf16[1,2,2112,128]{3,2,1,0:T(8,128)(2,1)S(1)}, bf16[1,2,2112,128]{3,2,1,0:T(8,128)(2,1)S(1)}, u32[]{:S(2)}, u32[]{:S(2)}) collective-permute-start(bf16[1,2,2112,128]{3,2,1,0:T(8,128)(2,1)S(1)} %get-tuple-element.414), channel_id=1, source_target_pairs={{3,0},{0,1},{1,2},{2,3},{7,4},{4,5},{5,6},{6,7},{11,8},{8,9},{9,10... | collective-permute-start | bytes 3244040 | tf_op jit(solution)/shard_map/while/body/eval_jaxpr/ppermute | solution.py:21
  224.1 25.5 %collective-permute-start = (bf16[1,2,2112,128]{3,2,1,0:T(8,128)(2,1)S(1)}, bf16[1,2,2112,128]{3,2,1,0:T(8,128)(2,1)S(1)}, u32[]{:S(2)}, u32[]{:S(2)}) collective-permute-start(bf16[1,2,2112,128]{3,2,1,0:T(8,128)(2,1)S(1)} %get-tuple-element.414), channel_id=1, source_target_pairs={{3,0},{0,1},{1,2},{2,3},{7,4},{4,5},{5,6},{6,7},{11,8},{8,9},{9,10... | collective-permute-start | bytes 3244040 | tf_op jit(solution)/shard_map/while/body/eval_jaxpr/ppermute | solution.py:21
Sparse Core Ops, SparseCore 0:
  90.1 22.5 all-gather.2
  118.0 31.2 reduce-scatter.1
where the time goes:
time: 275 us; the launch traced here: 274 us
  waiting for transfers between devices  128 us (47%)
  other arithmetic  59 us (21%)
  local copies, waits for them, and re-layouts  31 us (11%)
  blocking collectives  21.2 us (8%)
  matrix products  19.8 us (7%)
  between operations  14.3 us (5%)
    ppermute x3, waiting for transfers between devices, shifted(): return lax.ppermute(block, axis, route)  78 us
    unnamed x2, other arithmetic  46.5 us
    reduce_scatter x1, waiting for transfers between devices, local(): lax.psum_scatter(jnp.einsum('btd,dc->btc', spread, local_weights, preferr...  28.9 us
    all_gather x1, waiting for transfers between devices, local(): spread = lax.all_gather(sliced, 'wide', axis=1, tiled=True)  21.2 us
    all_to_all x1, blocking collectives, local(): lax.all_to_all(normed, 'blk', split_axis=2, concat_axis=0, tiled=True)  12.2 us
    unnamed x12, local copies, waits for them, and re-layouts  10.5 us
    all_to_all x1, blocking collectives, local(): lax.all_to_all(heads_out, 'wide', split_axis=1, concat_axis=2, tiled=True)  8.97 us
    reduce_sum x4, other arithmetic, attend(): total = total * decay + jnp.sum(weights, axis=1)  8.72 us
  transfers between devices with their start and end apart: 5, of which 5 were waited for; matrix products, arithmetic and copies ran while one was open for 1% of the time, Pallas kernels for 0%

commit v1 on v0

--- a/solution.py
+++ b/solution.py
@@ -80,7 +80,19 @@
     key_cols = lax.dynamic_slice_in_dim(key_weight_matrix, head_base, HEAD_WIDTH, 1)
     value_cols = lax.dynamic_slice_in_dim(value_weight_matrix, head_base, HEAD_WIDTH, 1)
     kv_width = key_cols.shape[1]
-    sliced = lax.all_to_all(normed, "blk", split_axis=2, concat_axis=0, tiled=True)
+    ways, here = (lax.axis_size("blk"), lax.axis_index("blk"))
+    width = normed.shape[2] // ways
+    shape = list(normed.shape)
+    shape[2] = width
+    height = shape[0]
+    shape[0] = height * ways
+    full = jnp.zeros(shape, normed.dtype)
+    for mask in range(ways):
+        part = lax.dynamic_slice_in_dim(normed, (here ^ mask) * width, width, axis=2)
+        if mask:
+            part = lax.ppermute(part, "blk", [(d, d ^ mask) for d in range(ways)])
+        full = lax.dynamic_update_slice_in_dim(full, part, (here ^ mask) * height, axis=0)
+    sliced = full
     spread = lax.all_gather(sliced, "wide", axis=1, tiled=True)
     local_weights = jnp.concatenate([w_query, key_cols, value_cols], axis=1)
     summed = lax.psum_scatter(

time: 275 us -> 205 us (0.75)
  other arithmetic: 59 us -> 14.1 us
  local copies, waits for them, and re-layouts: 31 us -> 8.32 us
  blocking collectives: 21.2 us -> 8.91 us
  starting transfers between devices: 0.4 us -> 5.9 us
  waiting for transfers between devices: 128 us -> 133 us
    unnamed x2 -> x1, other arithmetic: 46.5 us -> 1.38 us
    all_to_all x1 -> x0, blocking collectives: 12.2 us -> none  [local(): lax.all_to_all(normed, 'blk', split_axis=2, concat_axis=0, tiled=True)]
    all_to_all x1 -> x0, local copies, waits for them, and re-layouts: 8.57 us -> none  [local(): lax.all_to_all(normed, 'blk', split_axis=2, concat_axis=0, tiled=True)]
    unnamed x12, local copies, waits for them, and re-layouts: 10.5 us -> 3.1 us
    convert_element_type x1 -> x0, local copies, waits for them, and re-layouts: 6.74 us -> none  [local(): normed = (tokens * inv_rms * norm_gain[None, :]).astype(jnp.bfloat16)[None]]
    ppermute x0 -> x3, starting transfers between devices: none -> 5.68 us  [local(): part = lax.ppermute(part, 'blk', [(d, d ^ mask) for d in range(ways)])]
    ppermute x0 -> x3, waiting for transfers between devices: none -> 5.62 us  [local(): part = lax.ppermute(part, 'blk', [(d, d ^ mask) for d in range(ways)])]
  transfers between devices with their start and end apart: 5 -> 8, of which waited for: 5 -> 7; matrix products, arithmetic and copies ran while one was open for 1% -> 2% of each run, Pallas kernels for 0% -> 0%
where the time goes in v1:
time: 205 us
  waiting for transfers between devices  133 us (65%)
  matrix products  19.8 us (10%)
  between operations  14.3 us (7%)
  other arithmetic  14.1 us (7%)
  blocking collectives  8.91 us (4%)
  local copies, waits for them, and re-layouts  8.32 us (4%)
  starting transfers between devices  5.9 us (3%)
    ppermute x3, waiting for transfers between devices, shifted(): return lax.ppermute(block, axis, route)  78 us
    reduce_scatter x1, waiting for transfers between devices, local(): lax.psum_scatter(jnp.einsum('btd,dc->btc', spread, local_weights, preferr...  28.9 us
    all_gather x1, waiting for transfers between devices, local(): spread = lax.all_gather(sliced, 'wide', axis=1, tiled=True)  20.5 us
    all_to_all x1, blocking collectives, local(): lax.all_to_all(heads_out, 'wide', split_axis=1, concat_axis=2, tiled=True)  8.91 us
    reduce_sum x4, other arithmetic, attend(): total = total * decay + jnp.sum(weights, axis=1)  8.9 us
    dot_general x4, matrix products, attend(): jnp.dot(weights.astype(jnp.bfloat16), values_flat, preferred_element_type...  8.44 us
    dot_general x4, matrix products, attend(): lax.dot_general(queries, keys_flat, (((1,), (1,)), ((), ())), preferred_e...  6.25 us
    ppermute x3, starting transfers between devices, local(): part = lax.ppermute(part, 'blk', [(d, d ^ mask) for d in range(ways)])  5.68 us
  transfers between devices with their start and end apart: 8, of which 7 were waited for; matrix products, arithmetic and copies ran while one was open for 2% of the time, Pallas kernels for 0%

profile of v1, /device:TPU:0, one launch (start us, length us, event | category | flops | bytes accessed | tf_op | source)
XLA Modules:
  0.0 204.6 jit_solution(726903121814875002)
XLA Ops:
  6.5 1.1 fusion.31
  7.6 1.0 fusion.33
  8.7 3.1 %collective-permute-start.1 = (bf16[1,8,2048]{2,1,0:T(8,128)(2,1)S(1)}, bf16[1,8,2048]{2,1,0:T(8,128)(2,1)S(1)}, u32[]{:S(2)}, u32[]{:S(2)}) collective-permute-start(bf16[1,8,2048]{2,1,0:T(8,128)(2,1)S(1)} %get-tuple-element.309), channel_id=1, source_target_pairs={{0,1},{1,0},{2,3},{3,2},{4,5},{5,4},{6,7},{7,6},{8,9},{9,8},{10,11... | collective-permute-start | bytes 98312 | tf_op jit(solution)/shard_map/ppermute | solution.py:93
  11.8 2.6 %collective-permute-start.2 = (bf16[1,8,2048]{2,1,0:T(8,128)(2,1)S(1)}, bf16[1,8,2048]{2,1,0:T(8,128)(2,1)S(1)}, u32[]{:S(2)}, u32[]{:S(2)}) collective-permute-start(bf16[1,8,2048]{2,1,0:T(8,128)(2,1)S(1)} %get-tuple-element.308), channel_id=1, source_target_pairs={{0,2},{1,3},{2,0},{3,1},{4,6},{5,7},{6,4},{7,5},{8,10},{9,11},{10,... | collective-permute-start | bytes 98312 | tf_op jit(solution)/shard_map/ppermute | solution.py:93
  14.4 2.7 %collective-permute-done.2 = bf16[1,8,2048]{2,1,0:T(8,128)(2,1)S(1)} collective-permute-done((bf16[1,8,2048]{2,1,0:T(8,128)(2,1)S(1)}, bf16[1,8,2048]{2,1,0:T(8,128)(2,1)S(1)}, u32[]{:S(2)}, u32[]{:S(2)}) %collective-permute-start.2) | collective-permute-done | bytes 32800 | tf_op jit(solution)/shard_map/ppermute | solution.py:93
  17.2 2.9 %collective-permute-done.3 = bf16[1,8,2048]{2,1,0:T(8,128)(2,1)S(1)} collective-permute-done((bf16[1,8,2048]{2,1,0:T(8,128)(2,1)S(1)}, bf16[1,8,2048]{2,1,0:T(8,128)(2,1)S(1)}, u32[]{:S(2)}, u32[]{:S(2)}) %collective-permute-start.3) | collective-permute-done | bytes 32800 | tf_op jit(solution)/shard_map/ppermute | solution.py:93
  20.8 1.3 constant_dynamic-slice_fusion.2
  22.2 20.5 %all-gather.2.cloned.1.call-done = bf16[4,64,2048]{2,1,0:T(8,128)(2,1)} async-done(((bf16[4,8,2048]{2,1,0:T(8,128)(2,1)}), bf16[4,64,2048]{2,1,0:T(8,128)(2,1)}) %all-gather.2.cloned.1.call-update) | async-done | bytes 1048592 | tf_op jit(solution)/shard_map/all_gather | solution.py:96
  42.6 5.1 %fusion.16 = f32[4,64,1280]{2,1,0:T(8,128)} fusion(bf16[4,64,2048]{2,1,0:T(8,128)(2,1)} %all-gather.2.cloned.1.call-done, bf16[2048,128]{1,0:T(8,128)(2,1)S(1)} %get-tuple-element.322, bf16[2048,128]{1,0:T(8,128)(2,1)S(1)} %get-tuple-element.323, bf16[2048,1024]{1,0:T(8,128)(2,1)} %param.14), kind=kOutput, calls=%fused_computation.23 | convolution fusion | flops 1357905920 | bytes 7602176 | tf_op jit(solution)/shard_map/btd,dc->btc/dot_general | solution.py:99
  49.0 1.3 constant_dynamic-slice_fusion
  50.3 28.9 %reduce-scatter.2.cloned.1.call-done = f32[1,64,1280]{2,1,0:T(8,128)} async-done(((f32[4,64,1280]{2,1,0:T(8,128)}), f32[1,64,1280]{2,1,0:T(8,128)}) %reduce-scatter.2.cloned.1.call-update) | async-done | bytes 327696 | tf_op jit(solution)/shard_map/reduce_scatter | solution.py:98
  79.2 0.8 slice_bitcast_fusion.9
  79.9 0.8 slice.89
  80.7 1.0 slice_bitcast_fusion.8
  82.5 1.6 fusion.56
  84.1 2.4 %fusion.23 = f32[512]{0:T(512)S(1)} fusion(f32[512,2112]{0,1:T(8,128)S(1)} %get-tuple-element.317, f32[512]{0:T(512)S(1)} %broadcast_maximum_fusion, pred[2112]{0:T(1024)(128)(4,1)S(1)} %fusion.46, s32[512]{0:T(512)S(1)} %sub.128, s32[512]{0:T(512)S(1)} %le.68, s32[2112]{0:T(1024)S(1)} %get-tuple-element.318), kind=kLoop, calls=%fused_computation.33 | loop fusion | flops 7568896 | bytes 4344128 | tf_op jit(solution)/shard_map/reduce_sum | solution.py:159
  86.4 2.0 fusion.28
  88.5 97.3 %while.22 = (s32[]{:T(128)}, f32[512]{0:T(512)S(1)}, f32[512]{0:T(512)S(1)}, f32[512,128]{1,0:T(8,128)S(1)}, bf16[1,2,2112,128]{3,2,1,0:T(8,128)(2,1)S(1)}, /*in...) while((s32[]{:T(128)}, f32[512]{0:T(512)S(1)}, ...), condition=%wide.region_9.10_spmd.clone, body=%wide.region_5.9_spmd.clone.sunk | while | flops 576570880 | bytes 21332160 | solution.py:179
  88.9 26.9 %collective-permute-done = bf16[1,2,2112,128]{3,2,1,0:T(8,128)(2,1)S(1)} collective-permute-done((bf16[1,2,2112,128]{3,2,1,0:T(8,128)(2,1)S(1)}, bf16[1,2,2112,128]{3,2,1,0:T(8,128)(2,1)S(1)}, u32[]{:S(2)}, u32[]{:S(2)}) %collective-permute-start) | collective-permute-done | bytes 1081376 | tf_op jit(solution)/shard_map/while/body/eval_jaxpr/ppermute | solution.py:21
  115.8 1.6 fusion.69
  117.4 2.2 %fusion.70 = f32[512]{0:T(512)S(1)} fusion(f32[512,2112]{0,1:T(8,128)S(1)} %get-tuple-element.392, f32[512]{0:T(512)S(1)} %max.20, pred[2112]{0:T(1024)(128)(4,1)S(1)} %fusion.68, s32[512]{0:T(512)S(1)} %ge.93, s32[512]{0:T(512)S(1)} %le.136, s32[2112]{0:T(1024)S(1)} %add_select_fusion.3), kind=kLoop, calls=%fused_computation.7.clone.1 | loop fusion | flops 7568896 | bytes 4344128 | tf_op jit(solution)/shard_map/while/body/eval_jaxpr/reduce_sum | solution.py:159
  119.7 2.1 %fusion.71 = f32[512,128]{1,0:T(8,128)S(1)} fusion(f32[512,2112]{0,1:T(8,128)S(1)} %get-tuple-element.392, f32[512]{0:T(512)S(1)} %max.20, bf16[1,2,2112,128]{3,2,1,0:T(8,128)(2,1)S(1)} %collective-permute-done, f32[512,128]{1,0:T(8,128)S(1)} %get-tuple-element.416, f32[512]{0:T(512)S(1)} %get-tuple-element.394, s32[512]{0:T(512)S(1)} %ge.93, ...), kind=kOutput, calls=%fused_computation.11.clone.1 | convolution fusion | flops 284524544 | bytes 5413888 | tf_op jit(solution)/shard_map/while/body/eval_jaxpr/dot_general | solution.py:160
  122.2 26.0 %collective-permute-done = bf16[1,2,2112,128]{3,2,1,0:T(8,128)(2,1)S(1)} collective-permute-done((bf16[1,2,2112,128]{3,2,1,0:T(8,128)(2,1)S(1)}, bf16[1,2,2112,128]{3,2,1,0:T(8,128)(2,1)S(1)}, u32[]{:S(2)}, u32[]{:S(2)}) %collective-permute-start) | collective-permute-done | bytes 1081376 | tf_op jit(solution)/shard_map/while/body/eval_jaxpr/ppermute | solution.py:21
  148.2 1.6 fusion.69
  149.8 2.2 %fusion.70 = f32[512]{0:T(512)S(1)} fusion(f32[512,2112]{0,1:T(8,128)S(1)} %get-tuple-element.392, f32[512]{0:T(512)S(1)} %max.20, pred[2112]{0:T(1024)(128)(4,1)S(1)} %fusion.68, s32[512]{0:T(512)S(1)} %ge.93, s32[512]{0:T(512)S(1)} %le.136, s32[2112]{0:T(1024)S(1)} %add_select_fusion.3), kind=kLoop, calls=%fused_computation.7.clone.1 | loop fusion | flops 7568896 | bytes 4344128 | tf_op jit(solution)/shard_map/while/body/eval_jaxpr/reduce_sum | solution.py:159
  152.1 2.1 %fusion.71 = f32[512,128]{1,0:T(8,128)S(1)} fusion(f32[512,2112]{0,1:T(8,128)S(1)} %get-tuple-element.392, f32[512]{0:T(512)S(1)} %max.20, bf16[1,2,2112,128]{3,2,1,0:T(8,128)(2,1)S(1)} %collective-permute-done, f32[512,128]{1,0:T(8,128)S(1)} %get-tuple-element.416, f32[512]{0:T(512)S(1)} %get-tuple-element.394, s32[512]{0:T(512)S(1)} %ge.93, ...), kind=kOutput, calls=%fused_computation.11.clone.1 | convolution fusion | flops 284524544 | bytes 5413888 | tf_op jit(solution)/shard_map/while/body/eval_jaxpr/dot_general | solution.py:160
  154.6 25.1 %collective-permute-done = bf16[1,2,2112,128]{3,2,1,0:T(8,128)(2,1)S(1)} collective-permute-done((bf16[1,2,2112,128]{3,2,1,0:T(8,128)(2,1)S(1)}, bf16[1,2,2112,128]{3,2,1,0:T(8,128)(2,1)S(1)}, u32[]{:S(2)}, u32[]{:S(2)}) %collective-permute-start) | collective-permute-done | bytes 1081376 | tf_op jit(solution)/shard_map/while/body/eval_jaxpr/ppermute | solution.py:21
  179.7 1.6 fusion.69
  181.3 2.2 %fusion.70 = f32[512]{0:T(512)S(1)} fusion(f32[512,2112]{0,1:T(8,128)S(1)} %get-tuple-element.392, f32[512]{0:T(512)S(1)} %max.20, pred[2112]{0:T(1024)(128)(4,1)S(1)} %fusion.68, s32[512]{0:T(512)S(1)} %ge.93, s32[512]{0:T(512)S(1)} %le.136, s32[2112]{0:T(1024)S(1)} %add_select_fusion.3), kind=kLoop, calls=%fused_computation.7.clone.1 | loop fusion | flops 7568896 | bytes 4344128 | tf_op jit(solution)/shard_map/while/body/eval_jaxpr/reduce_sum | solution.py:159
  183.6 2.1 %fusion.71 = f32[512,128]{1,0:T(8,128)S(1)} fusion(f32[512,2112]{0,1:T(8,128)S(1)} %get-tuple-element.392, f32[512]{0:T(512)S(1)} %max.20, bf16[1,2,2112,128]{3,2,1,0:T(8,128)(2,1)S(1)} %collective-permute-done, f32[512,128]{1,0:T(8,128)S(1)} %get-tuple-element.416, f32[512]{0:T(512)S(1)} %get-tuple-element.394, s32[512]{0:T(512)S(1)} %ge.93, ...), kind=kOutput, calls=%fused_computation.11.clone.1 | convolution fusion | flops 284524544 | bytes 5413888 | tf_op jit(solution)/shard_map/while/body/eval_jaxpr/dot_general | solution.py:160
  186.6 1.4 reduce.7
  188.0 8.9 %all_to_all.18 = bf16[8,2,4096]{2,1,0:T(2,128)(2,1)S(1)} all-to-all(bf16[8,2,4096]{2,1,0:T(2,128)(2,1)S(1)} %reshape.407), channel_id=1, replica_groups=mesh['wide'=8,'blk'=4] {'wide'}, dimensions={0} | all-to-all | bytes 262144 | tf_op jit(solution)/shard_map/all_to_all | solution.py:187
  (88 shorter events, 5.2 us)
Async XLA Ops:
  6.5 36.1 %all-gather.2.cloned.1.call-start = ((), (), s32[]{:S(2)}) async-start(), calls=%async_computation.2 | async-start | bytes 1179648 | tf_op jit(solution)/shard_map/all_gather | solution.py:96
  8.7 5.7 %collective-permute-start.1 = (bf16[1,8,2048]{2,1,0:T(8,128)(2,1)S(1)}, bf16[1,8,2048]{2,1,0:T(8,128)(2,1)S(1)}, u32[]{:S(2)}, u32[]{:S(2)}) collective-permute-start(bf16[1,8,2048]{2,1,0:T(8,128)(2,1)S(1)} %get-tuple-element.309), channel_id=1, source_target_pairs={{0,1},{1,0},{2,3},{3,2},{4,5},{5,4},{6,7},{7,6},{8,9},{9,8},{10,11... | collective-permute-start | bytes 98312 | tf_op jit(solution)/shard_map/ppermute | solution.py:93
  11.8 5.4 %collective-permute-start.2 = (bf16[1,8,2048]{2,1,0:T(8,128)(2,1)S(1)}, bf16[1,8,2048]{2,1,0:T(8,128)(2,1)S(1)}, u32[]{:S(2)}, u32[]{:S(2)}) collective-permute-start(bf16[1,8,2048]{2,1,0:T(8,128)(2,1)S(1)} %get-tuple-element.308), channel_id=1, source_target_pairs={{0,2},{1,3},{2,0},{3,1},{4,6},{5,7},{6,4},{7,5},{8,10},{9,11},{10,... | collective-permute-start | bytes 98312 | tf_op jit(solution)/shard_map/ppermute | solution.py:93
  14.4 5.7 %collective-permute-start.3 = (bf16[1,8,2048]{2,1,0:T(8,128)(2,1)S(1)}, bf16[1,8,2048]{2,1,0:T(8,128)(2,1)S(1)}, u32[]{:S(2)}, u32[]{:S(2)}) collective-permute-start(bf16[1,8,2048]{2,1,0:T(8,128)(2,1)S(1)} %get-tuple-element.307), channel_id=1, source_target_pairs={{0,3},{1,2},{2,1},{3,0},{4,7},{5,6},{6,5},{7,4},{8,11},{9,10},{10,... | collective-permute-start | bytes 98312 | tf_op jit(solution)/shard_map/ppermute | solution.py:93
  20.1 0.7 copy-start
  20.8 58.4 %reduce-scatter.2.cloned.1.call-start = ((), (), s32[]{:S(2)}) async-start(), calls=%async_computation.3 | async-start | bytes 1638400 | tf_op jit(solution)/shard_map/reduce_scatter | solution.py:98
  42.6 5.8 %copy-start.2 = (s32[1,64]{1,0:T(1,128)S(1)}, s32[1,64]{1,0:T(1,128)}, u32[]{:S(2)}) copy-start(s32[1,64]{1,0:T(1,128)} %param.20) | copy-start | bytes 772
  42.6 6.0 %copy-start.1 = (s32[16]{0:T(128)S(1)}, s32[16]{0:T(128)}, u32[]{:S(2)}) copy-start(s32[16]{0:T(128)} %param.21) | copy-start | bytes 196
  88.5 27.3 %collective-permute-start = (bf16[1,2,2112,128]{3,2,1,0:T(8,128)(2,1)S(1)}, bf16[1,2,2112,128]{3,2,1,0:T(8,128)(2,1)S(1)}, u32[]{:S(2)}, u32[]{:S(2)}) collective-permute-start(bf16[1,2,2112,128]{3,2,1,0:T(8,128)(2,1)S(1)} %get-tuple-element.417), channel_id=1, source_target_pairs={{3,0},{0,1},{1,2},{2,3},{7,4},{4,5},{5,6},{6,7},{11,8},{8,9},{9,10... | collective-permute-start | bytes 3244040 | tf_op jit(solution)/shard_map/while/body/eval_jaxpr/ppermute | solution.py:21
  121.8 26.4 %collective-permute-start = (bf16[1,2,2112,128]{3,2,1,0:T(8,128)(2,1)S(1)}, bf16[1,2,2112,128]{3,2,1,0:T(8,128)(2,1)S(1)}, u32[]{:S(2)}, u32[]{:S(2)}) collective-permute-start(bf16[1,2,2112,128]{3,2,1,0:T(8,128)(2,1)S(1)} %get-tuple-element.417), channel_id=1, source_target_pairs={{3,0},{0,1},{1,2},{2,3},{7,4},{4,5},{5,6},{6,7},{11,8},{8,9},{9,10... | collective-permute-start | bytes 3244040 | tf_op jit(solution)/shard_map/while/body/eval_jaxpr/ppermute | solution.py:21
  154.2 25.5 %collective-permute-start = (bf16[1,2,2112,128]{3,2,1,0:T(8,128)(2,1)S(1)}, bf16[1,2,2112,128]{3,2,1,0:T(8,128)(2,1)S(1)}, u32[]{:S(2)}, u32[]{:S(2)}) collective-permute-start(bf16[1,2,2112,128]{3,2,1,0:T(8,128)(2,1)S(1)} %get-tuple-element.417), channel_id=1, source_target_pairs={{3,0},{0,1},{1,2},{2,3},{7,4},{4,5},{5,6},{6,7},{11,8},{8,9},{9,10... | collective-permute-start | bytes 3244040 | tf_op jit(solution)/shard_map/while/body/eval_jaxpr/ppermute | solution.py:21
Sparse Core Ops, SparseCore 0:
  20.9 21.6 all-gather.1
  47.9 31.2 reduce-scatter.1
